TPU v7x, 32 devices: a whole 2x2x4 slice. The times are simulated.
32 devices in a mesh: seq: 4 (over y, x), chan: 8 (over z, core).
Axes of the slice: x: 2, y: 2, z: 4, core: 2. Of those that a mesh axis runs over, the one named last changes fastest.
Arguments:
- conv_input: bfloat16 [4096, 4096], P('seq', 'chan'), may hold values from -0.0078125 to 0.0078125
- grad_out: bfloat16 [4096, 4096], P(('seq', 'chan')), may hold values from -6 to 6
- out_weight: bfloat16 [4096, 4096], P('chan'), may hold values from -0.09375 to 0.09375
- filters: bfloat16 [128, 8192], P('chan'), may hold values from -0.0625 to 0.0625
Outputs:
- grad_input: bfloat16 [4096, 4096], P('seq', 'chan')
- grad_filters: float32 [128, 8192], P('chan', 'seq')
All inputs are finite; a program needn't handle non-finite values.
Results may differ from a plain program's by a relative error of at most 0.0051.
Values may be sent and summed in bfloat16 or wider, within the bound.
A program may use at most 512 MiB of HBM per device.

v0:
```python
import jax
import jax.numpy as jnp
from jax import lax
from jax.sharding import PartitionSpec as P

BLK = 128


def toeplitz_tile(vector, tile_rows):
    group_count = vector.shape[0]
    spread = jnp.broadcast_to(vector[:, None, :], (group_count, tile_rows, 2 * tile_rows))
    flat_rows = spread.reshape(group_count, 2 * tile_rows * tile_rows)[
        :, : tile_rows * (2 * tile_rows - 1)
    ]
    return flat_rows.reshape(group_count, tile_rows, 2 * tile_rows - 1)[:, :, tile_rows - 1 :]


def diagonal_sums(products):
    group_count = products.shape[0]
    tile_rows = products.shape[1]
    flipped = jnp.pad(products[:, ::-1, :], ((0, 0), (0, 0), (0, tile_rows)))
    flat_rows = flipped.reshape(group_count, 2 * tile_rows * tile_rows)[
        :, : tile_rows * (2 * tile_rows - 1)
    ]
    return jnp.sum(flat_rows.reshape(group_count, tile_rows, 2 * tile_rows - 1), axis=1)


def tile_stack(filter_rows, offset_count):
    group_count = filter_rows.shape[0]
    padded_filter = jnp.pad(filter_rows, ((0, 0), (BLK, 5 * BLK)))
    blocks = padded_filter[:, 1 : 1 + (offset_count + 1) * BLK].reshape(
        group_count, offset_count + 1, BLK
    )
    vectors = jnp.concatenate([blocks[:, :-1], blocks[:, 1:]], axis=2)
    tiles = toeplitz_tile(vectors.reshape(group_count * offset_count, 2 * BLK), BLK)
    return tiles.reshape(group_count, offset_count, BLK, BLK).transpose(1, 0, 2, 3)


def channel_grads(input_major, later_major, filter_rows):
    group_count = filter_rows.shape[0]
    lag_count = filter_rows.shape[1]
    group_width = input_major.shape[0] // group_count
    row_count = input_major.shape[1]
    block_count = row_count // BLK
    offset_count = lag_count // BLK + 4
    tiles = tile_stack(filter_rows, offset_count)
    input_tiles = input_major.reshape(group_count, group_width, block_count, BLK)

    def one_offset(grad_acc, items):
        offset, matrix = items
        window = lax.dynamic_slice_in_dim(later_major, offset * BLK, row_count, 1)
        window = window.reshape(group_count, group_width, block_count, BLK)
        grad_acc = grad_acc + jnp.einsum(
            "gsr,gcar->gcas", matrix, window, preferred_element_type=jnp.float32
        )
        products = jnp.einsum(
            "gcas,gcar->gsr", input_tiles, window, preferred_element_type=jnp.float32
        )
        return (grad_acc, products)

    start_acc = jnp.zeros((group_count, group_width, block_count, BLK), jnp.float32)
    offsets = jnp.arange(offset_count, dtype=jnp.int32)
    grad_acc, products = lax.scan(one_offset, start_acc, (offsets, tiles), unroll=4)
    stacked = products.transpose(1, 0, 2, 3).reshape(group_count * offset_count, BLK, BLK)
    sums = jnp.pad(diagonal_sums(stacked), ((0, 0), (0, 1)))
    sums = sums.reshape(group_count, offset_count, 2, BLK)
    total = jnp.pad(sums[:, :, 0], ((0, 0), (0, 1), (0, 0))) + jnp.pad(
        sums[:, :, 1], ((0, 0), (1, 0), (0, 0))
    )
    flat_total = total.reshape(group_count, (offset_count + 1) * BLK)
    return (
        grad_acc.reshape(group_count * group_width, row_count),
        flat_total[:, BLK - 1 : BLK - 1 + lag_count],
    )


def on_device(conv_input, grad_out, out_weight, filters):
    grad_major = lax.dot_general(
        out_weight,
        lax.all_gather(grad_out, "chan", axis=0, tiled=True),
        (((1,), (1,)), ((), ())),
        preferred_element_type=jnp.float32,
    ).astype(jnp.bfloat16)
    lag_count = filters.shape[1]
    input_major = conv_input.T
    seq_count = lax.axis_size("seq")
    wide_input, wide_grad = (
        lax.all_to_all(input_major, "seq", split_axis=0, concat_axis=1, tiled=True),
        lax.all_to_all(grad_major, "seq", split_axis=0, concat_axis=1, tiled=True),
    )
    local_groups = filters.shape[0] // seq_count
    own_filters = lax.dynamic_slice_in_dim(
        filters, lax.axis_index("seq") * local_groups, local_groups, 0
    )
    later_major = jnp.pad(wide_grad, ((0, 0), (0, lag_count + 4 * BLK)))
    grad_wide, filter_part = channel_grads(wide_input, later_major, own_filters)
    grad_back = lax.all_to_all(
        grad_wide.astype(jnp.bfloat16), "seq", split_axis=1, concat_axis=0, tiled=True
    )
    grad_input = grad_back.T
    grad_filters = lax.all_to_all(filter_part, "seq", split_axis=1, concat_axis=0, tiled=True)
    return (grad_input, grad_filters)


def solution(mesh):
    in_specs = (P("seq", "chan"), P(("seq", "chan"), None), P("chan", None), P("chan", None))
    out_specs = (P("seq", "chan"), P("chan", "seq"))
    return jax.shard_map(
        on_device, mesh=mesh, in_specs=in_specs, out_specs=out_specs, check_vma=False
    )
```

profile of v0, /device:TPU:0, one launch (start us, length us, event | category | flops | bytes accessed | tf_op | source)
XLA Modules:
  0.0 923.3 jit_solution(13668629579575706574)
XLA Ops:
  10.2 5.2 all-to-all-start.1
  15.5 79.0 %all-gather.2.cloned.1.call-done = bf16[1024,4096]{1,0:T(8,128)(2,1)} async-done(((bf16[128,4096]{1,0:T(8,128)(2,1)}), bf16[1024,4096]{1,0:T(8,128)(2,1)}) %all-gather.2.cloned.1.call-update) | async-done | bytes 8388624 | tf_op jit(solution)/shard_map/all_gather | solution.py:80
  94.4 10.1 %convolution_convert_fusion = bf16[512,1024]{1,0:T(8,128)(2,1)} fusion(bf16[512,4096]{1,0:T(8,128)(2,1)} %param.8, bf16[1024,4096]{1,0:T(8,128)(2,1)} %all-gather.2.cloned.1.call-done), kind=kOutput, calls=%fused_computation.34 | convolution fusion | flops 4295491584 | bytes 13631488 | tf_op jit(solution)/shard_map/dot_general | solution.py:78
  104.6 3.7 all-to-all-start
  111.1 44.3 %copy.79 = bf16[34,8,128,256]{3,1,2,0:T(8,128)(2,1)S(1)} copy(bf16[34,8,128,256]{3,2,1,0:T(8,128)(2,1)S(1)} %bitcast.225) | data formatting | bytes 35651584
  155.4 7.0 slice.78
  162.4 60.1 %reshape.105 = bf16[272,128,255]{2,1,0:T(8,128)(2,1)} reshape(bf16[272,32640]{1,0:T(8,128)(2,1)} %slice.78) | data formatting | bytes 35512320 | tf_op jit(solution)/shard_map/reshape | solution.py:15
  222.5 10.5 %slice.79 = bf16[272,128,128]{2,1,0:T(8,128)(2,1)} slice(bf16[272,128,255]{2,1,0:T(8,128)(2,1)} %reshape.105), slice={[0:272], [0:128], [127:255]} | slice | bytes 17825792 | tf_op jit(solution)/shard_map/slice | solution.py:15
  235.4 372.5 %while.13 = (s32[]{:T(128)}, f32[4,32,32,128]{3,2,1,0:T(8,128)}, f32[17,4,4,128,128]{4,3,1,0,2:T(8,128)}, s32[17,4]{0,1:T(4,128)S(1)}, bf16[128,12800]{1,0:T(8,1...) while((s32[]{:T(128)}, f32[4,32,32,128]{3,2,1,0:T(8,128)}, ...), condition=%wide.region_1.2_spmd.clone, body=%wide.region_0.1_spmd.clone.sunk | while | flops 1077149696 | bytes 100139752 | solution.py:63
  245.6 2.5 copy.95
  289.4 2.5 copy.95
  333.2 2.5 copy.95
  355.1 2.5 copy.95
  398.9 2.5 copy.95
  608.0 134.5 %rev.3 = f32[272,128,128]{2,1,0:T(8,128)} reverse(f32[272,128,128]{2,1,0:T(8,128)} %bitcast.227), dimensions={1} | reverse | bytes 35651584 | tf_op jit(solution)/shard_map/rev | solution.py:21
  742.5 9.9 %pad.26 = f32[272,128,256]{2,1,0:T(8,128)S(1)} pad(f32[272,128,128]{2,1,0:T(8,128)} %rev.3, f32[]{:T(128)} %constant.34.clone.1), padding=0_0x0_0x0_128 | pad | bytes 53477380 | tf_op jit(solution)/shard_map/jit(_pad)/pad | solution.py:21
  752.4 39.5 %copy.80 = f32[34,8,128,256]{3,1,2,0:T(8,128)} copy(f32[34,8,128,256]{3,2,1,0:T(8,128)S(1)} %bitcast.215) | data formatting | bytes 71303168
  791.9 25.3 %slice.80 = f32[272,32640]{1,0:T(8,128)} slice(f32[272,32768]{1,0:T(8,128)} %bitcast.216), slice={[0:272], [0:32640]} | slice | bytes 71024640 | tf_op jit(solution)/shard_map/slice | solution.py:22
  817.2 58.2 %reshape.112 = f32[272,128,255]{2,1,0:T(8,128)} reshape(f32[272,32640]{1,0:T(8,128)} %slice.80) | data formatting | bytes 71024640 | tf_op jit(solution)/shard_map/reshape | solution.py:25
  875.4 12.8 %reduce_sum.9 = f32[272,255]{1,0:T(8,128)S(1)} reduce(f32[272,128,255]{2,1,0:T(8,128)} %reshape.112, f32[]{:T(128)} %constant.34.clone.1), dimensions={1}, to_apply=%region_2.3 | reduce | flops 8808720 | bytes 35789764 | tf_op jit(solution)/shard_map/reduce_sum | solution.py:25
  889.5 4.2 all-to-all-start.3
  895.9 2.8 all-to-all-done.3
  898.7 3.5 all-to-all-start.2
  902.9 11.7 %all-to-all-done.2 = bf16[128,4,1024]{0,2,1:T(8,128)(2,1)S(1)} async-done(((bf16[128,4,1024]{0,2,1:T(8,128)(2,1)}), bf16[128,4,1024]{0,2,1:T(8,128)(2,1)S(1)}, u32[]{:S(2)}, u32[]{:S(2)}) %all-to-all-start.2) | async-done | bytes 1048608 | tf_op jit(solution)/shard_map/all_to_all | solution.py:97
  (645 shorter events, 328.0 us)
Async XLA Ops:
  7.2 8.2 copy-start
  7.2 87.2 %all-gather.2.cloned.1.call-start = ((), (), s32[]{:S(2)}) async-start(), calls=%async_computation.4 | async-start | bytes 9437184 | tf_op jit(solution)/shard_map/all_gather | solution.py:80
  10.2 94.3 %all-to-all-start.1 = ((bf16[4,128,1024]{2,1,0:T(8,128)(2,1)}), bf16[4,128,1024]{2,1,0:T(8,128)(2,1)S(1)}, u32[]{:S(2)}, u32[]{:S(2)}) async-start(bf16[4,128,1024]{2,1,0:T(8,128)(2,1)} %bitcast.6), calls=%async_computation.1 | async-start | bytes 2097152 | tf_op jit(solution)/shard_map/all_to_all | solution.py:88
  104.6 130.6 %all-to-all-start = ((bf16[4,128,1024]{2,1,0:T(8,128)(2,1)}), bf16[4,128,1024]{2,1,0:T(8,128)(2,1)S(1)}, u32[]{:S(2)}, u32[]{:S(2)}) async-start(bf16[4,128,1024]{2,1,0:T(8,128)(2,1)} %bitcast), calls=%async_computation | async-start | bytes 2097152 | tf_op jit(solution)/shard_map/all_to_all | solution.py:89
  250.0 5.7 copy-start.5
  271.9 5.7 copy-start.5
  293.8 5.7 copy-start.5
  315.7 5.7 copy-start.5
  337.6 5.7 copy-start.5
  359.5 5.7 copy-start.5
  381.4 5.7 copy-start.5
  403.3 5.7 copy-start.5
  425.2 5.7 copy-start.5
  447.1 5.7 copy-start.5
  469.0 5.7 copy-start.5
  490.9 5.7 copy-start.5
  534.8 5.7 copy-start.5
  556.7 5.7 copy-start.5
  578.6 5.7 copy-start.5
  600.5 5.7 copy-start.5
  875.4 18.3 %copy-start.10 = (f32[4,32,32,128]{3,2,1,0:T(8,128)S(1)}, f32[4,32,32,128]{3,2,1,0:T(8,128)}, u32[]{:S(2)}) copy-start(f32[4,32,32,128]{3,2,1,0:T(8,128)} %get-tuple-element.40) | copy-start | bytes 6291460
  888.2 28.3 %copy-start.1 = (bf16[16,8192]{1,0:T(8,128)(2,1)S(1)}, bf16[16,8192]{1,0:T(8,128)(2,1)}, u32[]{:S(2)}) copy-start(bf16[16,8192]{1,0:T(8,128)(2,1)} %param.9) | copy-start | bytes 786436
  889.5 9.2 all-to-all-start.3
  898.7 15.9 %all-to-all-start.2 = ((bf16[128,4,1024]{0,2,1:T(8,128)(2,1)}), bf16[128,4,1024]{0,2,1:T(8,128)(2,1)S(1)}, u32[]{:S(2)}, u32[]{:S(2)}) async-start(bf16[128,4,1024]{0,2,1:T(8,128)(2,1)} %copy.47), calls=%async_computation.2 | async-start | bytes 2097152 | tf_op jit(solution)/shard_map/all_to_all | solution.py:97
  (137 other events, 356.3 us)
Sparse Core Ops, SparseCore 0:
  9.6 84.7 all-gather.1
where the time goes:
time: 936 us; the launch traced here: 923 us
  local copies, waits for them, and re-layouts  552 us (59%)
  matrix products  170 us (18%)
  waiting for transfers between devices  94.1 us (10%)
  loops' own time  46.1 us (5%)
  other arithmetic  30.6 us (3%)
  starting transfers between devices  16.6 us (2%)
  between operations  14.2 us (2%)
    rev x1, local copies, waits for them, and re-layouts, diagonal_sums(): flipped = jnp.pad(products[:, ::-1, :], ((0, 0), (0, 0), (0, tile_rows)))  135 us
    dot_general x68, matrix products, one_offset(): jnp.einsum('gsr,gcar->gcas', matrix, window, preferred_element_type=jnp.f...  127 us
    unnamed x11, local copies, waits for them, and re-layouts  85.2 us
    all_gather x1, waiting for transfers between devices, on_device(): lax.all_gather(grad_out, 'chan', axis=0, tiled=True)  79 us
    while x391, local copies, waits for them, and re-layouts  75.2 us
    dynamic_update_slice x34, local copies, waits for them, and re-layouts, channel_grads(): lax.scan(one_offset, start_acc, (offsets, tiles), unroll=4)  63.1 us
    reshape x1, local copies, waits for them, and re-layouts, toeplitz_tile(): flat_rows.reshape(group_count, tile_rows, 2 * tile_rows - 1)  60.1 us
    reshape x1, local copies, waits for them, and re-layouts, diagonal_sums(): flat_rows.reshape(group_count, tile_rows, 2 * tile_rows - 1)  58.2 us
  transfers between devices with their start and end apart: 5, of which 3 were waited for; matrix products, arithmetic and copies ran while one was open for 15% of the time, Pallas kernels for 0%

commit v1 on v0

v1 whole, which is shorter than its diff:
```python
import functools

import jax
import jax.numpy as jnp
from jax import lax
from jax.experimental import pallas as pl
from jax.experimental.pallas import tpu as pltpu
from jax.sharding import PartitionSpec as P

HALF = 128
BLK = 2 * HALF
SUB = 8


def conv_kernel(width, gm_ref, x_ref, f_ref, gi_ref, gf_ref, toep, prod, gm_rows, x_cols):
    groups = f_ref.shape[0]
    rows = gm_ref.shape[1]
    lags = f_ref.shape[2]
    used = min(lags, rows)
    count = rows // BLK
    span = rows + HALF
    depth = count * width

    @pl.loop(0, groups)
    def _(g):
        first = pl.multiple_of(g * width, width)

        taps = f_ref[g, :, :used]
        pieces = [jnp.zeros((1, HALF), jnp.float32), taps]
        if used < rows:
            pieces.append(jnp.zeros((1, rows - used), jnp.float32))
        line = jnp.concatenate(pieces, axis=1)
        base = jnp.concatenate(
            [line] + [pltpu.roll(line, r, 1) for r in range(1, SUB)], axis=0
        )
        for k in range(0, HALF // SUB, 2):
            low = base if k == 0 else pltpu.roll(base, k * SUB, 1)
            high = pltpu.roll(base, (k + 1) * SUB, 1)
            both = jnp.concatenate([low, high], axis=0).astype(jnp.bfloat16)
            toep[k * SUB : (k + 2) * SUB, HALF:] = both[:, HALF:]
        toep[:, :HALF] = jnp.zeros((HALF, HALF), jnp.bfloat16)

        for a in range(count):
            gm_rows[a * width : (a + 1) * width, :] = gm_ref[
                pl.ds(first, width), a * BLK : (a + 1) * BLK
            ]
        gm_rows[depth:, :] = jnp.zeros((gm_rows.shape[0] - depth, BLK), jnp.bfloat16)
        x_rows = jnp.concatenate(
            [x_ref[pl.ds(first, width), a * BLK : (a + 1) * BLK] for a in range(count)], axis=0
        )
        x_cols[...] = x_rows.T

        step = min(4, count)
        total = None
        for j in range(0, count, step):
            m = (count - j) * width
            left = jnp.concatenate(
                [gm_rows[(j + q) * width : (j + q) * width + m, :] for q in range(step)], axis=1
            )
            right = jnp.concatenate(
                [
                    toep[:, HALF + j * BLK : HALF + (j + step) * BLK],
                    toep[:, j * BLK : (j + step) * BLK],
                ],
                axis=0,
            )
            part = lax.dot_general(
                left, right, (((1,), (1,)), ((), ())), preferred_element_type=jnp.float32
            )
            if total is None:
                total = part
            else:
                total = jnp.concatenate([total[:m] + part, total[m:]], axis=0)
        for a in range(count):
            gi_ref[pl.ds(first, width), a * BLK : (a + 1) * BLK] = total[
                a * width : (a + 1) * width
            ].astype(jnp.bfloat16)

        prod[:, :HALF] = jnp.zeros((HALF, HALF), jnp.float32)
        for j in range(count):
            k = min(depth, -(-((count - j) * width) // BLK) * BLK)
            part = jnp.dot(
                x_cols[:, :k],
                gm_rows[j * width : j * width + k, :],
                preferred_element_type=jnp.float32,
            )
            lo = j * BLK
            if j:
                prod[:, lo : lo + HALF] += part[HALF:, :HALF]
            prod[:, lo + HALF : lo + BLK] = part[:HALF, :HALF] + part[HALF:, HALF:]
            prod[:, lo + BLK : lo + BLK + HALF] = part[:HALF, HALF:]
        acc = prod[:SUB, :]
        for k in range(1, HALF // SUB):
            acc = acc + pltpu.roll(prod[k * SUB : (k + 1) * SUB, :], span - k * SUB, 1)
        out = acc[:1]
        for r in range(1, SUB):
            out = out + pltpu.roll(acc[r : r + 1], span - r, 1)
        gf_ref[g, :, :used] = out[:, HALF : HALF + used]
        if used < lags:
            gf_ref[g, :, used:] = jnp.zeros((1, lags - used), jnp.float32)


def conv_grads(gm_major, x_major, filter_rows):
    groups, lags = filter_rows.shape
    channels, rows = gm_major.shape
    width = channels // groups
    depth = rows // BLK * width
    grad_wide, filter_part = pl.pallas_call(
        functools.partial(conv_kernel, width),
        out_shape=(
            jax.ShapeDtypeStruct((channels, rows), jnp.bfloat16),
            jax.ShapeDtypeStruct((groups, 1, lags), jnp.float32),
        ),
        in_specs=[pl.BlockSpec(memory_space=pltpu.VMEM)] * 3,
        out_specs=(pl.BlockSpec(memory_space=pltpu.VMEM),) * 2,
        scratch_shapes=[
            pltpu.VMEM((HALF, rows + HALF), jnp.bfloat16),
            pltpu.VMEM((HALF, rows + HALF), jnp.float32),
            pltpu.VMEM((2 * depth, BLK), jnp.bfloat16),
            pltpu.VMEM((BLK, depth), jnp.bfloat16),
        ],
        compiler_params=pltpu.CompilerParams(vmem_limit_bytes=48 * 1024 * 1024),
    )(gm_major, x_major, filter_rows.astype(jnp.float32).reshape(groups, 1, lags))
    return grad_wide, filter_part.reshape(groups, lags)


def on_device(conv_input, grad_out, out_weight, filters):
    grad_major = lax.dot_general(
        out_weight,
        lax.all_gather(grad_out, "chan", axis=0, tiled=True),
        (((1,), (1,)), ((), ())),
        preferred_element_type=jnp.float32,
    ).astype(jnp.bfloat16)
    seq_count = lax.axis_size("seq")
    wide_input = lax.all_to_all(conv_input.T, "seq", split_axis=0, concat_axis=1, tiled=True)
    wide_grad = lax.all_to_all(grad_major, "seq", split_axis=0, concat_axis=1, tiled=True)
    local_groups = filters.shape[0] // seq_count
    own_filters = lax.dynamic_slice_in_dim(
        filters, lax.axis_index("seq") * local_groups, local_groups, 0
    )
    grad_wide, filter_part = conv_grads(wide_grad, wide_input, own_filters)
    grad_back = lax.all_to_all(grad_wide, "seq", split_axis=1, concat_axis=0, tiled=True)
    grad_filters = lax.all_to_all(filter_part, "seq", split_axis=1, concat_axis=0, tiled=True)
    return (grad_back.T, grad_filters)


def solution(mesh):
    in_specs = (P("seq", "chan"), P(("seq", "chan"), None), P("chan", None), P("chan", None))
    out_specs = (P("seq", "chan"), P("chan", "seq"))
    return jax.shard_map(
        on_device, mesh=mesh, in_specs=in_specs, out_specs=out_specs, check_vma=False
    )
```

time: 936 us -> 166 us (0.18); the launches traced: 923 us -> 165 us
  local copies, waits for them, and re-layouts: 552 us -> 5.65 us
  matrix products: 170 us -> 10.1 us
  loops' own time: 46.1 us -> 0 us
  other arithmetic: 30.6 us -> 1.92 us
  waiting for transfers between devices: 94.1 us -> 108 us
  Pallas kernels: 0 us -> 9.72 us
    dot_general x136 -> x0, matrix products: 160 us -> none  [the longest x68 127 us: one_offset(): jnp.einsum('gsr,gcar->gcas', matrix, window, preferred_element_type=jnp.f...]
    rev x1 -> x0, local copies, waits for them, and re-layouts: 135 us -> none  [diagonal_sums(): flipped = jnp.pad(products[:, ::-1, :], ((0, 0), (0, 0), (0, tile_rows)))]
    reshape x5 -> x1, local copies, waits for them, and re-layouts: 120 us -> 0.09 us  [conv_grads(): filter_rows.astype(jnp.float32).reshape(groups, 1, lags)]
    unnamed x11 -> x0, local copies, waits for them, and re-layouts: 85.2 us -> none
    while x391 -> x0, local copies, waits for them, and re-layouts: 75.2 us -> none
    dynamic_update_slice x34 -> x0, local copies, waits for them, and re-layouts: 63.1 us -> none  [channel_grads(): lax.scan(one_offset, start_acc, (offsets, tiles), unroll=4)]
    slice x24 -> x0, local copies, waits for them, and re-layouts: 53.5 us -> none  [the longest x1 25.3 us: diagonal_sums(): flipped.reshape(group_count, 2 * tile_rows * tile_rows)]
    another operation x1 -> x0, loops' own time: 46.1 us -> none  [channel_grads(): lax.scan(one_offset, start_acc, (offsets, tiles), unroll=4)]
  transfers between devices with their start and end apart: 5 -> 5, of which waited for: 3 -> 4; matrix products, arithmetic and copies ran while one was open for 15% -> 9% of each run, Pallas kernels for 0% -> 0%
where the time goes in v1:
time: 166 us; the launch traced here: 165 us
  waiting for transfers between devices  108 us (65%)
  starting transfers between devices  15.7 us (9%)
  between operations  14.1 us (8%)
  matrix products  10.1 us (6%)
  Pallas kernels  9.72 us (6%)
  local copies, waits for them, and re-layouts  5.65 us (3%)
  other arithmetic  1.92 us (1%)
    all_gather x1, waiting for transfers between devices, on_device(): lax.all_gather(grad_out, 'chan', axis=0, tiled=True)  79 us
    all_to_all x1, waiting for transfers between devices, on_device(): lax.all_to_all(grad_major, 'seq', split_axis=0, concat_axis=1, tiled=True)  13 us
    all_to_all x1, waiting for transfers between devices, on_device(): lax.all_to_all(grad_wide, 'seq', split_axis=1, concat_axis=0, tiled=True)  11.4 us
    dot_general x1, matrix products, on_device(): lax.dot_general(out_weight, lax.all_gather(grad_out, 'chan', axis=0, tile...  10.1 us
    pallas_call x1, Pallas kernels, conv_grads(): pl.pallas_call(functools.partial(conv_kernel, width), out_shape=(jax.Shap...  9.72 us
    all_to_all x1, starting transfers between devices, on_device(): lax.all_to_all(conv_input.T, 'seq', split_axis=0, concat_axis=1, tiled=True)  5.16 us
    all_to_all x1, waiting for transfers between devices, on_device(): lax.all_to_all(filter_part, 'seq', split_axis=1, concat_axis=0, tiled=True)  3.93 us
    all_to_all x1, starting transfers between devices, on_device(): lax.all_to_all(grad_major, 'seq', split_axis=0, concat_axis=1, tiled=True)  3.69 us
  transfers between devices with their start and end apart: 5, of which 4 were waited for; matrix products, arithmetic and copies ran while one was open for 9% of the time, Pallas kernels for 0%

profile of v1, /device:TPU:0, one launch (start us, length us, event | category | flops | bytes accessed | tf_op | source)
XLA Modules:
  0.0 165.3 jit_solution(16468591123018988014)
XLA Ops:
  7.2 0.0 all-gather.2.cloned.1.call-start
  7.2 0.7 all-gather.2.cloned.1.call-update
  7.9 2.3 %copy.11 = bf16[512,1024]{1,0:T(8,128)(2,1)} copy(bf16[512,1024]{0,1:T(8,128)(2,1)} %bitcast.27) | data formatting | bytes 2097152 | tf_op jit(solution)/shard_map/transpose | solution.py:135
  10.2 5.2 %all-to-all-start.1 = ((bf16[4,128,1024]{2,1,0:T(8,128)(2,1)}), bf16[4,128,1024]{2,1,0:T(8,128)(2,1)S(1)}, u32[]{:S(2)}, u32[]{:S(2)}) async-start(bf16[4,128,1024]{2,1,0:T(8,128)(2,1)} %bitcast.3), calls=%async_computation.1 | async-start | bytes 2097152 | tf_op jit(solution)/shard_map/all_to_all | solution.py:135
  15.4 79.0 %all-gather.2.cloned.1.call-done = bf16[1024,4096]{1,0:T(8,128)(2,1)} async-done(((bf16[128,4096]{1,0:T(8,128)(2,1)}), bf16[1024,4096]{1,0:T(8,128)(2,1)}) %all-gather.2.cloned.1.call-update) | async-done | bytes 8388624 | tf_op jit(solution)/shard_map/all_gather | solution.py:130
  94.4 10.1 %convolution_convert_fusion = bf16[512,1024]{1,0:T(8,128)(2,1)} fusion(bf16[512,4096]{1,0:T(8,128)(2,1)} %param.6, bf16[1024,4096]{1,0:T(8,128)(2,1)} %all-gather.2.cloned.1.call-done), kind=kOutput, calls=%fused_computation | convolution fusion | flops 4295491584 | bytes 13631488 | tf_op jit(solution)/shard_map/dot_general | solution.py:128
  104.5 0.0 all-to-all-done.1
  104.5 3.7 %all-to-all-start = ((bf16[4,128,1024]{2,1,0:T(8,128)(2,1)}), bf16[4,128,1024]{2,1,0:T(8,128)(2,1)S(1)}, u32[]{:S(2)}, u32[]{:S(2)}) async-start(bf16[4,128,1024]{2,1,0:T(8,128)(2,1)} %bitcast), calls=%async_computation | async-start | bytes 2097152 | tf_op jit(solution)/shard_map/all_to_all | solution.py:136
  108.2 0.9 dynamic-slice_convert_fusion
  109.2 0.1 reshape.26.f_ref
  109.3 0.1 copy.18
  109.4 13.0 %all-to-all-done = bf16[4,128,1024]{2,1,0:T(8,128)(2,1)S(1)} async-done(((bf16[4,128,1024]{2,1,0:T(8,128)(2,1)}), bf16[4,128,1024]{2,1,0:T(8,128)(2,1)S(1)}, u32[]{:S(2)}, u32[]{:S(2)}) %all-to-all-start) | async-done | bytes 1048608 | tf_op jit(solution)/shard_map/all_to_all | solution.py:136
  122.4 0.1 copy.17
  122.5 9.7 %shard_map.59 = (bf16[128,4096]{1,0:T(8,128)(2,1)S(1)}, f32[4,1,8192]{2,1,0:T(1,128)S(1)}) custom-call(bf16[128,4096]{1,0:T(8,128)(2,1)S(1)} %bitcast.22, bf16[128,4096]{1,0:T(8,128)(2,1)S(1)} %bitcast.21, f32[4,1,8192]{2,1,0:T(1,128)S(1)} %reshape.26.f_ref), custom_call_target="tpu_custom_call" | custom-call | tf_op jit(solution)/shard_map/pallas_call | solution.py:108
  132.2 1.0 reduce
  133.2 3.3 %all-to-all-start.3 = ((f32[4,4,2048]{2,0,1:T(4,128)}), f32[4,4,2048]{2,0,1:T(4,128)S(1)}, u32[]{:S(2)}, u32[]{:S(2)}) async-start(f32[4,4,2048]{2,0,1:T(4,128)} %bitcast.10), calls=%async_computation.3 | async-start | bytes 262144 | tf_op jit(solution)/shard_map/all_to_all | solution.py:143
  136.5 1.1 copy.20
  137.6 3.9 %all-to-all-done.3 = f32[4,4,2048]{2,0,1:T(4,128)S(1)} async-done(((f32[4,4,2048]{2,0,1:T(4,128)}), f32[4,4,2048]{2,0,1:T(4,128)S(1)}, u32[]{:S(2)}, u32[]{:S(2)}) %all-to-all-start.3) | async-done | bytes 131104 | tf_op jit(solution)/shard_map/all_to_all | solution.py:143
  141.5 3.5 %all-to-all-start.2 = ((bf16[128,4,1024]{2,0,1:T(8,128)(2,1)}), bf16[128,4,1024]{2,0,1:T(8,128)(2,1)S(1)}, u32[]{:S(2)}, u32[]{:S(2)}) async-start(bf16[128,4,1024]{2,0,1:T(8,128)(2,1)} %bitcast.20), calls=%async_computation.2 | async-start | bytes 2097152 | tf_op jit(solution)/shard_map/all_to_all | solution.py:142
  145.0 0.7 all_to_all.71
  145.7 11.4 %all-to-all-done.2 = bf16[128,4,1024]{2,0,1:T(8,128)(2,1)S(1)} async-done(((bf16[128,4,1024]{2,0,1:T(8,128)(2,1)}), bf16[128,4,1024]{2,0,1:T(8,128)(2,1)S(1)}, u32[]{:S(2)}, u32[]{:S(2)}) %all-to-all-start.2) | async-done | bytes 1048608 | tf_op jit(solution)/shard_map/all_to_all | solution.py:142
  157.1 1.3 copy.14
Async XLA Ops:
  7.2 87.2 %all-gather.2.cloned.1.call-start = ((), (), s32[]{:S(2)}) async-start(), calls=%async_computation.4 | async-start | bytes 9437184 | tf_op jit(solution)/shard_map/all_gather | solution.py:130
  10.2 94.3 %all-to-all-start.1 = ((bf16[4,128,1024]{2,1,0:T(8,128)(2,1)}), bf16[4,128,1024]{2,1,0:T(8,128)(2,1)S(1)}, u32[]{:S(2)}, u32[]{:S(2)}) async-start(bf16[4,128,1024]{2,1,0:T(8,128)(2,1)} %bitcast.3), calls=%async_computation.1 | async-start | bytes 2097152 | tf_op jit(solution)/shard_map/all_to_all | solution.py:135
  104.5 17.8 %all-to-all-start = ((bf16[4,128,1024]{2,1,0:T(8,128)(2,1)}), bf16[4,128,1024]{2,1,0:T(8,128)(2,1)S(1)}, u32[]{:S(2)}, u32[]{:S(2)}) async-start(bf16[4,128,1024]{2,1,0:T(8,128)(2,1)} %bitcast), calls=%async_computation | async-start | bytes 2097152 | tf_op jit(solution)/shard_map/all_to_all | solution.py:136
  133.2 8.3 %all-to-all-start.3 = ((f32[4,4,2048]{2,0,1:T(4,128)}), f32[4,4,2048]{2,0,1:T(4,128)S(1)}, u32[]{:S(2)}, u32[]{:S(2)}) async-start(f32[4,4,2048]{2,0,1:T(4,128)} %bitcast.10), calls=%async_computation.3 | async-start | bytes 262144 | tf_op jit(solution)/shard_map/all_to_all | solution.py:143
  141.5 15.6 %all-to-all-start.2 = ((bf16[128,4,1024]{2,0,1:T(8,128)(2,1)}), bf16[128,4,1024]{2,0,1:T(8,128)(2,1)S(1)}, u32[]{:S(2)}, u32[]{:S(2)}) async-start(bf16[128,4,1024]{2,0,1:T(8,128)(2,1)} %bitcast.20), calls=%async_computation.2 | async-start | bytes 2097152 | tf_op jit(solution)/shard_map/all_to_all | solution.py:142
Sparse Core Ops, SparseCore 0:
  9.6 84.7 all-gather.1

commit v2 on v1

v2 whole, which is shorter than its diff:
```python
import functools

import jax
import jax.numpy as jnp
from jax import lax
from jax.experimental import pallas as pl
from jax.experimental.pallas import tpu as pltpu
from jax.sharding import PartitionSpec as P

HALF = 128
BLK = 2 * HALF
SUB = 8

MESH = pl.DeviceIdType.MESH
PARTS = 2


def whole_kernel(
    chan_count, seq_count, width,
    x_hbm, go_hbm, w_hbm, f_ref,
    gi_out, gf_out,
    gath, w_vm, x_vm, x_turn, x_major, taps, toep, x_cols, gm_send, gm_wide, gm_rows,
    gi_send, gi_back, prod, gf_send, gf_back,
    load_sem, hop_send, hop_recv, x_send, x_recv, gm_ssem, gm_rsem, gi_ssem, gi_rsem, gf_ssem, gf_rsem,
):
    chips = chan_count // 2
    seq = lax.axis_index("seq")
    chan = lax.axis_index("chan")
    spot = chan // 2
    core = lax.rem(chan, 2)
    tok = go_hbm.shape[0]
    piece = tok // PARTS
    span_t = x_hbm.shape[0]
    rows = span_t * seq_count
    groups = f_ref.shape[0] // seq_count
    lags = f_ref.shape[1]
    used = min(lags, rows)
    own_ch = groups * width
    unit = 2 * tok
    count = rows // BLK
    span = rows + HALF
    depth = count * width
    cut = lags // seq_count

    up = {"chan": chan + 2}
    down = {"chan": chan - 2}
    twin = {"chan": chan + 1 - 2 * core}
    has_up = spot < chips - 1
    has_down = spot > 0

    def peer(r):
        return lax.rem(seq + r, seq_count)

    barrier = pltpu.get_barrier_semaphore()
    pl.semaphore_signal(barrier, inc=1, device_id=twin, device_id_type=MESH)
    for r in range(1, seq_count):
        pl.semaphore_signal(barrier, inc=1, device_id={"seq": peer(r)}, device_id_type=MESH)

    @pl.when(has_up)
    def _():
        pl.semaphore_signal(barrier, inc=1, device_id=up, device_id_type=MESH)

    @pl.when(has_down)
    def _():
        pl.semaphore_signal(barrier, inc=1, device_id=down, device_id_type=MESH)

    load_own = pltpu.make_async_copy(
        go_hbm, gath.at[spot, pl.ds(core * tok, tok)], load_sem.at[0]
    )
    load_own.start()
    load_x = pltpu.make_async_copy(x_hbm, x_vm, load_sem.at[1])
    load_x.start()
    load_w = pltpu.make_async_copy(w_hbm, w_vm, load_sem.at[2])
    load_w.start()

    @pl.when(has_up & has_down)
    def _():
        pl.semaphore_wait(barrier, seq_count + 2)

    @pl.when(jnp.logical_not(has_up & has_down))
    def _():
        pl.semaphore_wait(barrier, seq_count + min(chips - 1, 1))

    def slot(q, side, h):
        return gath.at[q, pl.ds(pl.multiple_of(side * tok + h * piece, piece), piece)]

    def hop(way, q, h, target):
        return pltpu.make_async_remote_copy(
            src_ref=slot(q, core, h),
            dst_ref=slot(q, core, h),
            send_sem=hop_send.at[way, q, h],
            recv_sem=hop_recv.at[q, core, h],
            device_id=target,
            device_id_type=MESH,
        )

    def arrived(q, side, h):
        pltpu.make_async_remote_copy(
            src_ref=slot(q, side, h),
            dst_ref=slot(q, side, h),
            send_sem=hop_send.at[2, q, h],
            recv_sem=hop_recv.at[q, side, h],
            device_id=twin,
            device_id_type=MESH,
        ).wait_recv()

    load_own.wait()
    for h in range(PARTS):
        @pl.when(has_up)
        def _():
            hop(0, spot, h, up).start()

        @pl.when(has_down)
        def _():
            hop(1, spot, h, down).start()

    for h in range(PARTS):
        hop(2, spot, h, twin).start()

    load_x.wait()
    for i in range(0, x_vm.shape[1], HALF):
        x_turn[i : i + HALF, :] = x_vm[:, i : i + HALF].T

    def x_copy(source, target):
        return pltpu.make_async_remote_copy(
            src_ref=x_turn.at[pl.ds(pl.multiple_of(target * own_ch, own_ch), own_ch)],
            dst_ref=x_major.at[source],
            send_sem=x_send.at[target],
            recv_sem=x_recv.at[source],
            device_id={"seq": target},
            device_id_type=MESH,
        )

    for r in range(1, seq_count):
        x_copy(seq, peer(r)).start()
    x_major[seq] = x_turn[pl.ds(pl.multiple_of(seq * own_ch, own_ch), own_ch), :]

    for i in range(f_ref.shape[0]):
        taps[i] = f_ref[i : i + 1, :used].astype(jnp.float32)

    @pl.loop(0, groups)
    def _(g):
        pieces = [jnp.zeros((1, HALF), jnp.float32), taps[seq * groups + g]]
        if used < rows:
            pieces.append(jnp.zeros((1, rows - used), jnp.float32))
        line = jnp.concatenate(pieces, axis=1)
        base = jnp.concatenate(
            [line] + [pltpu.roll(line, r, 1) for r in range(1, SUB)], axis=0
        )
        for k in range(0, HALF // SUB, 2):
            low = base if k == 0 else pltpu.roll(base, k * SUB, 1)
            high = pltpu.roll(base, (k + 1) * SUB, 1)
            both = jnp.concatenate([low, high], axis=0).astype(jnp.bfloat16)
            toep[g, k * SUB : (k + 2) * SUB, HALF:] = both[:, HALF:]
        toep[g, :, :HALF] = jnp.zeros((HALF, HALF), jnp.bfloat16)

    def gm_copy(q, source, target):
        return pltpu.make_async_remote_copy(
            src_ref=gm_send.at[q, pl.ds(pl.multiple_of(target * own_ch, own_ch), own_ch)],
            dst_ref=gm_wide.at[source * chips + q],
            send_sem=gm_ssem.at[q, target],
            recv_sem=gm_rsem.at[q, source],
            device_id={"seq": target},
            device_id_type=MESH,
        )

    def project(q):
        for h in range(PARTS):
            arrived(q, 1 - core, h)
        gm_send[q] = lax.dot_general(
            w_vm[...], gath[q], (((1,), (1,)), ((), ())), preferred_element_type=jnp.float32
        ).astype(jnp.bfloat16)
        for r in range(1, seq_count):
            gm_copy(q, seq, peer(r)).start()
        gm_wide[seq * chips + q] = gm_send[
            q, pl.ds(pl.multiple_of(seq * own_ch, own_ch), own_ch), :
        ]

    load_w.wait()
    for r in range(1, seq_count):
        x_copy(peer(r), seq).wait_recv()

    @pl.loop(0, groups)
    def _(g):
        first = pl.multiple_of(g * width, width)
        per = span_t // BLK
        x_rows = jnp.concatenate(
            [
                x_major[a // per, pl.ds(first, width), (a % per) * BLK : (a % per + 1) * BLK]
                for a in range(count)
            ],
            axis=0,
        )
        x_cols[g] = x_rows.T

    def relay(d):
        for h in range(PARTS):
            @pl.when(spot >= d)
            def _():
                arrived(spot - d, core, h)

                @pl.when(has_up)
                def _():
                    hop(0, spot - d, h, up).start()

                hop(2, spot - d, h, twin).start()

            @pl.when(spot + d < chips)
            def _():
                arrived(spot + d, core, h)

                @pl.when(has_down)
                def _():
                    hop(1, spot + d, h, down).start()

                hop(2, spot + d, h, twin).start()

    @pl.loop(0, chips)
    def _(d):
        @pl.when(d > 0)
        def _():
            relay(d)

        @pl.loop(0, 2)
        def _(side):
            q = spot - d + 2 * d * side

            @pl.when((q >= 0) & (q < chips) & (d + 1 - side > 0))
            def _():
                project(q)

    @pl.loop(0, chips)
    def _(q):
        for r in range(1, seq_count):
            gm_copy(q, peer(r), seq).wait_recv()

    def gi_copy(g, source, target):
        return pltpu.make_async_remote_copy(
            src_ref=gi_send.at[target, g],
            dst_ref=gi_back.at[source, g],
            send_sem=gi_ssem.at[g, target],
            recv_sem=gi_rsem.at[g, source],
            device_id={"seq": target},
            device_id_type=MESH,
        )

    def gf_copy(source, target):
        return pltpu.make_async_remote_copy(
            src_ref=gf_send.at[target],
            dst_ref=gf_back.at[source],
            send_sem=gf_ssem.at[target],
            recv_sem=gf_rsem.at[source],
            device_id={"seq": target},
            device_id_type=MESH,
        )

    @pl.loop(0, groups)
    def _(g):
        first = pl.multiple_of(g * width, width)
        fold = BLK // unit
        for a in range(count):
            for u in range(fold):
                gm_rows[a * width : (a + 1) * width, u * unit : (u + 1) * unit] = gm_wide[
                    a * fold + u, pl.ds(first, width), :
                ]
        gm_rows[depth:, :] = jnp.zeros((gm_rows.shape[0] - depth, BLK), jnp.bfloat16)

        step = min(4, count)
        total = None
        for j in range(0, count, step):
            m = (count - j) * width
            left = jnp.concatenate(
                [gm_rows[(j + q) * width : (j + q) * width + m, :] for q in range(step)], axis=1
            )
            right = jnp.concatenate(
                [
                    toep[g, :, HALF + j * BLK : HALF + (j + step) * BLK],
                    toep[g, :, j * BLK : (j + step) * BLK],
                ],
                axis=0,
            )
            part = lax.dot_general(
                left, right, (((1,), (1,)), ((), ())), preferred_element_type=jnp.float32
            )
            if total is None:
                total = part
            else:
                total = jnp.concatenate([total[:m] + part, total[m:]], axis=0)
        per = span_t // BLK
        for a in range(count):
            gi_send[a // per, g, :, (a % per) * BLK : (a % per + 1) * BLK] = total[
                a * width : (a + 1) * width
            ].astype(jnp.bfloat16)
        for r in range(1, seq_count):
            gi_copy(g, seq, peer(r)).start()
        gi_back[seq, g] = gi_send[seq, g]

        prod[:, :HALF] = jnp.zeros((HALF, HALF), jnp.float32)
        for j in range(count):
            k = min(depth, -(-((count - j) * width) // BLK) * BLK)
            part = jnp.dot(
                x_cols[g, :, :k],
                gm_rows[j * width : j * width + k, :],
                preferred_element_type=jnp.float32,
            )
            lo = j * BLK
            if j:
                prod[:, lo : lo + HALF] += part[HALF:, :HALF]
            prod[:, lo + HALF : lo + BLK] = part[:HALF, :HALF] + part[HALF:, HALF:]
            prod[:, lo + BLK : lo + BLK + HALF] = part[:HALF, HALF:]
        acc = prod[:SUB, :]
        for k in range(1, HALF // SUB):
            acc = acc + pltpu.roll(prod[k * SUB : (k + 1) * SUB, :], span - k * SUB, 1)
        out = acc[:1]
        for r in range(1, SUB):
            out = out + pltpu.roll(acc[r : r + 1], span - r, 1)
        for s in range(seq_count):
            live = min(max(used - s * cut, 0), cut)
            if live:
                gf_send[s, g, :, :live] = out[:, HALF + s * cut : HALF + s * cut + live]
            if live < cut:
                gf_send[s, g, :, live:] = jnp.zeros((1, cut - live), jnp.float32)

    for r in range(1, seq_count):
        gf_copy(seq, peer(r)).start()
    gf_back[seq] = gf_send[seq]

    @pl.loop(0, groups)
    def _(g):
        for r in range(1, seq_count):
            gi_copy(g, peer(r), seq).wait_recv()

    per_tile = max(1, HALF // own_ch)
    for s in range(0, seq_count, per_tile):
        tile = jnp.concatenate(
            [gi_back[s + i, g] for i in range(per_tile) for g in range(groups)], axis=0
        )
        gi_out[:, s * own_ch : (s + per_tile) * own_ch] = tile.T
    for r in range(1, seq_count):
        gf_copy(peer(r), seq).wait_recv()
    for s in range(seq_count):
        for g in range(groups):
            gf_out[s * groups + g : s * groups + g + 1, :] = gf_back[s, g]

    for r in range(1, seq_count):
        x_copy(seq, peer(r)).wait_send()
        gf_copy(seq, peer(r)).wait_send()

    @pl.loop(0, groups)
    def _(g):
        for r in range(1, seq_count):
            gi_copy(g, seq, peer(r)).wait_send()

    @pl.loop(0, chips)
    def _(q):
        for r in range(1, seq_count):
            gm_copy(q, seq, peer(r)).wait_send()
        for h in range(PARTS):
            hop(2, q, h, twin).wait_send()

            @pl.when(has_up & (q <= spot))
            def _():
                hop(0, q, h, up).wait_send()

            @pl.when(has_down & (q >= spot))
            def _():
                hop(1, q, h, down).wait_send()


def on_device(chan_count, seq_count, conv_input, grad_out, out_weight, filters):
    span_t, chans = conv_input.shape
    tok, model = grad_out.shape
    all_groups, lags = filters.shape
    width = chans // all_groups
    groups = all_groups // seq_count
    own_ch = groups * width
    rows = span_t * seq_count
    chips = chan_count // 2
    unit = 2 * tok
    count = rows // BLK
    depth = count * width
    cut = lags // seq_count
    used = min(lags, rows)
    bf16, f32 = jnp.bfloat16, jnp.float32
    dma = pltpu.SemaphoreType.DMA
    hbm = pl.BlockSpec(memory_space=pl.ANY)
    vmem = pl.BlockSpec(memory_space=pltpu.VMEM)
    work = chans * rows * model // seq_count + 2 * own_ch * rows * rows
    return pl.pallas_call(
        functools.partial(whole_kernel, chan_count, seq_count, width),
        out_shape=(
            jax.ShapeDtypeStruct((span_t, chans), bf16),
            jax.ShapeDtypeStruct((all_groups, cut), f32),
        ),
        in_specs=[hbm, hbm, hbm, vmem],
        out_specs=(vmem, vmem),
        scratch_shapes=[
            pltpu.VMEM((chips, unit, model), bf16),
            pltpu.VMEM(out_weight.shape, bf16),
            pltpu.VMEM((span_t, chans), bf16),
            pltpu.VMEM((chans, span_t), bf16),
            pltpu.VMEM((seq_count, own_ch, span_t), bf16),
            pltpu.VMEM((all_groups, 1, used), f32),
            pltpu.VMEM((groups, HALF, rows + HALF), bf16),
            pltpu.VMEM((groups, BLK, depth), bf16),
            pltpu.VMEM((chips, chans, unit), bf16),
            pltpu.VMEM((seq_count * chips, own_ch, unit), bf16),
            pltpu.VMEM((2 * depth, BLK), bf16),
            pltpu.VMEM((seq_count, groups, width, span_t), bf16),
            pltpu.VMEM((seq_count, groups, width, span_t), bf16),
            pltpu.VMEM((HALF, rows + HALF), f32),
            pltpu.VMEM((seq_count, groups, 1, cut), f32),
            pltpu.VMEM((seq_count, groups, 1, cut), f32),
            dma((3,)),
            dma((3, chips, PARTS)),
            dma((chips, 2, PARTS)),
            dma((seq_count,)),
            dma((seq_count,)),
            dma((chips, seq_count)),
            dma((chips, seq_count)),
            dma((groups, seq_count)),
            dma((groups, seq_count)),
            dma((seq_count,)),
            dma((seq_count,)),
        ],
        cost_estimate=pl.CostEstimate(
            flops=2 * work, bytes_accessed=16 * 1024 * 1024, transcendentals=0
        ),
        compiler_params=pltpu.CompilerParams(
            vmem_limit_bytes=56 * 1024 * 1024, collective_id=0, has_side_effects=True
        ),
    )(conv_input, grad_out, out_weight, filters)


def solution(mesh):
    in_specs = (P("seq", "chan"), P(("seq", "chan"), None), P("chan", None), P("chan", None))
    out_specs = (P("seq", "chan"), P("chan", "seq"))
    return jax.shard_map(
        functools.partial(on_device, mesh.shape["chan"], mesh.shape["seq"]),
        mesh=mesh, in_specs=in_specs, out_specs=out_specs, check_vma=False,
    )
```

time: 166 us -> 107 us (0.64)
  waiting for transfers between devices: 108 us -> 0 us
  Pallas kernels: 9.72 us -> 102 us
  starting transfers between devices: 15.7 us -> 0 us
  between operations: 14.1 us -> 0.64 us
  matrix products: 10.1 us -> 0 us
  other arithmetic: 1.92 us -> 0 us
  local copies, waits for them, and re-layouts: 5.65 us -> 3.83 us
    pallas_call x1, Pallas kernels: 9.72 us -> 102 us  [on_device(): pl.pallas_call(functools.partial(whole_kernel, chan_count, seq_count, wid...]
    all_gather x1 -> x0, waiting for transfers between devices: 79 us -> none  [on_device(): lax.all_gather(grad_out, 'chan', axis=0, tiled=True)]
    all_to_all x4 -> x0, waiting for transfers between devices: 28.3 us -> none  [the longest x1 13 us: on_device(): lax.all_to_all(grad_major, 'seq', split_axis=0, concat_axis=1, tiled=True)]
    all_to_all x4 -> x0, starting transfers between devices: 15.7 us -> none  [the longest x1 5.16 us: on_device(): lax.all_to_all(conv_input.T, 'seq', split_axis=0, concat_axis=1, tiled=True)]
    dot_general x1 -> x0, matrix products: 10.1 us -> none  [on_device(): lax.dot_general(out_weight, lax.all_gather(grad_out, 'chan', axis=0, tile...]
    unnamed x0 -> x2, local copies, waits for them, and re-layouts: none -> 3.83 us
    all_to_all x5 -> x0, local copies, waits for them, and re-layouts: 3.25 us -> none  [the longest x2 2.38 us: on_device(): lax.all_to_all(grad_wide, 'seq', split_axis=1, concat_axis=0, tiled=True)]
    transpose x1 -> x0, local copies, waits for them, and re-layouts: 2.31 us -> none  [on_device(): wide_input = lax.all_to_all(conv_input.T, 'seq', split_axis=0, concat_axi...]
  transfers between devices with their start and end apart: 5 -> 0, of which waited for: 4 -> 0; matrix products, arithmetic and copies ran while one was open for 9% -> 0% of each run, Pallas kernels for 0% -> 0%
where the time goes in v2:
time: 107 us; the launch traced here: 106 us
  Pallas kernels  102 us (95%)
  local copies, waits for them, and re-layouts  3.83 us (4%)
    pallas_call x1, Pallas kernels, on_device(): pl.pallas_call(functools.partial(whole_kernel, chan_count, seq_count, wid...  102 us
    unnamed x2, local copies, waits for them, and re-layouts  3.83 us

profile of v2, /device:TPU:0, one launch (start us, length us, event | category | flops | bytes accessed | tf_op | source)
XLA Modules:
  0.0 106.5 jit_solution(10871800047696437299)
XLA Ops:
  0.6 102.0 %shard_map.59 = (bf16[1024,512]{1,0:T(8,128)(2,1)}, f32[16,2048]{1,0:T(8,128)}) custom-call(bf16[1024,512]{1,0:T(8,128)(2,1)} %x_hbm.1, bf16[128,4096]{1,0:T(8,128)(2,1)} %go_hbm.1, bf16[512,4096]{1,0:T(8,128)(2,1)} %w_hbm.1, bf16[16,8192]{1,0:T(8,128)(2,1)} %f_ref.1), custom_call_target="tpu_custom_call" | custom-call | flops 12884901888 | bytes 16777216 | tf_op jit(solution)/shard_map/pallas_call | solution.py:389
  102.6 2.3 %copy.8 = bf16[1024,512]{1,0:T(8,128)(2,1)} copy(bf16[1024,512]{1,0:T(8,128)(2,1)} %get-tuple-element.4) | data formatting | bytes 2097152
  104.9 1.6 %copy.9 = f32[16,2048]{1,0:T(8,128)} copy(f32[16,2048]{1,0:T(8,128)} %get-tuple-element.5) | data formatting | bytes 262144

commit v3 on v2

--- a/solution.py
+++ b/solution.py
@@ -12,7 +12,7 @@
 SUB = 8
 
 MESH = pl.DeviceIdType.MESH
-PARTS = 2
+PARTS = 4
 
 
 def whole_kernel(
@@ -20,8 +20,8 @@
     x_hbm, go_hbm, w_hbm, f_ref,
     gi_out, gf_out,
     gath, w_vm, x_vm, x_turn, x_major, taps, toep, x_cols, gm_send, gm_wide, gm_rows,
-    gi_send, gi_back, prod, gf_send, gf_back,
-    load_sem, hop_send, hop_recv, x_send, x_recv, gm_ssem, gm_rsem, gi_ssem, gi_rsem, gf_ssem, gf_rsem,
+    gi_send, prod, gf_send, w_far, gm_far,
+    far_ssem, far_psem, far_rsem, far_gsem, own_sem, load_sem, hop_send, hop_recv, x_send, x_recv, gm_ssem, gm_rsem, gi_ssem, gi_rsem, gf_ssem, gf_rsem,
 ):
     chips = chan_count // 2
     seq = lax.axis_index("seq")
@@ -48,6 +48,21 @@
     has_up = spot < chips - 1
     has_down = spot > 0
 
+    upper = (2 * spot) // chips
+    edge = spot + upper * (chips - 1 - 2 * spot)
+    is_end = edge == 0 if chips >= 4 else spot < 0
+    is_inner = edge == 1 if chips >= 4 else spot < 0
+    mate = chan + (1 - 2 * upper) * (2 - 4 * edge)
+    far = (1 - upper) * (chips - 1)
+    far_parts = min(PARTS, own_ch // 16)
+    far_rows = own_ch // far_parts
+
+    def held(q):
+        return jnp.logical_not(is_end & (q == far))
+
+    def onward(q):
+        return jnp.logical_not(is_inner & (q == far))
+
     def peer(r):
         return lax.rem(seq + r, seq_count)
 
@@ -63,6 +78,13 @@
     @pl.when(has_down)
     def _():
         pl.semaphore_signal(barrier, inc=1, device_id=down, device_id_type=MESH)
+
+    @pl.when(is_end | is_inner)
+    def _():
+        for r in range(1, seq_count):
+            pl.semaphore_signal(
+                barrier, inc=1, device_id={"seq": peer(r), "chan": mate}, device_id_type=MESH
+            )
 
     load_own = pltpu.make_async_copy(
         go_hbm, gath.at[spot, pl.ds(core * tok, tok)], load_sem.at[0]
@@ -73,13 +95,19 @@
     load_w = pltpu.make_async_copy(w_hbm, w_vm, load_sem.at[2])
     load_w.start()
 
-    @pl.when(has_up & has_down)
+    greeted = seq_count - 1 if chips >= 4 else 0
+
+    @pl.when((edge == 1) & has_up & has_down)
+    def _():
+        pl.semaphore_wait(barrier, seq_count + 2 + greeted)
+
+    @pl.when((edge > 1) & has_up & has_down)
     def _():
         pl.semaphore_wait(barrier, seq_count + 2)
 
     @pl.when(jnp.logical_not(has_up & has_down))
     def _():
-        pl.semaphore_wait(barrier, seq_count + min(chips - 1, 1))
+        pl.semaphore_wait(barrier, seq_count + min(chips - 1, 1) + greeted)
 
     def slot(q, side, h):
         return gath.at[q, pl.ds(pl.multiple_of(side * tok + h * piece, piece), piece)]
@@ -104,6 +132,39 @@
             device_id_type=MESH,
         ).wait_recv()
 
+    def far_span(s, h):
+        return pl.ds(pl.multiple_of(s * own_ch + h * far_rows, far_rows), far_rows)
+
+    def far_hop(h):
+        return pltpu.make_async_remote_copy(
+            src_ref=w_hbm.at[far_span(seq, h)],
+            dst_ref=w_far.at[far_span(seq, h)],
+            send_sem=far_ssem.at[h],
+            recv_sem=far_rsem.at[seq, h],
+            device_id={"chan": mate},
+            device_id_type=MESH,
+        )
+
+    def far_share(source, target, h):
+        return pltpu.make_async_remote_copy(
+            src_ref=w_far.at[far_span(source, h)],
+            dst_ref=w_far.at[far_span(source, h)],
+            send_sem=far_psem.at[target, h],
+            recv_sem=far_rsem.at[source, h],
+            device_id={"seq": target},
+            device_id_type=MESH,
+        )
+
+    def far_gm(source, target):
+        return pltpu.make_async_remote_copy(
+            src_ref=gm_far.at[pl.ds(pl.multiple_of(target * own_ch, own_ch), own_ch)],
+            dst_ref=gm_wide.at[source * chips + far],
+            send_sem=far_gsem.at[target],
+            recv_sem=gm_rsem.at[far, source],
+            device_id={"seq": target, "chan": mate},
+            device_id_type=MESH,
+        )
+
     load_own.wait()
     for h in range(PARTS):
         @pl.when(has_up)
@@ -113,6 +174,11 @@
         @pl.when(has_down)
         def _():
             hop(1, spot, h, down).start()
+
+        if h < far_parts:
+            @pl.when(is_end)
+            def _():
+                far_hop(h).start()
 
     for h in range(PARTS):
         hop(2, spot, h, twin).start()
@@ -164,9 +230,17 @@
             device_id_type=MESH,
         )
 
+    def project_far():
+        for r in range(1, seq_count):
+            for h in range(far_parts):
+                far_share(peer(r), seq, h).wait_recv()
+        gm_far[...] = lax.dot_general(
+            w_far[...], gath[far], (((1,), (1,)), ((), ())), preferred_element_type=jnp.float32
+        ).astype(jnp.bfloat16)
+        for r in range(seq_count):
+            far_gm(seq, peer(r)).start()
+
     def project(q):
-        for h in range(PARTS):
-            arrived(q, 1 - core, h)
         gm_send[q] = lax.dot_general(
             w_vm[...], gath[q], (((1,), (1,)), ((), ())), preferred_element_type=jnp.float32
         ).astype(jnp.bfloat16)
@@ -195,25 +269,32 @@
 
     def relay(d):
         for h in range(PARTS):
-            @pl.when(spot >= d)
+            @pl.when((spot >= d) & held(spot - d))
             def _():
                 arrived(spot - d, core, h)
 
-                @pl.when(has_up)
+                @pl.when(has_up & onward(spot - d))
                 def _():
                     hop(0, spot - d, h, up).start()
 
                 hop(2, spot - d, h, twin).start()
 
-            @pl.when(spot + d < chips)
+            @pl.when((spot + d < chips) & held(spot + d))
             def _():
                 arrived(spot + d, core, h)
 
-                @pl.when(has_down)
+                @pl.when(has_down & onward(spot + d))
                 def _():
                     hop(1, spot + d, h, down).start()
 
                 hop(2, spot + d, h, twin).start()
+
+            if h < far_parts:
+                @pl.when(is_inner & (d == 1))
+                def _():
+                    far_hop(h).wait_recv()
+                    for r in range(1, seq_count):
+                        far_share(seq, peer(r), h).start()
 
     @pl.loop(0, chips)
     def _(d):
@@ -225,8 +306,15 @@
         def _(side):
             q = spot - d + 2 * d * side
 
-            @pl.when((q >= 0) & (q < chips) & (d + 1 - side > 0))
+            @pl.when((q >= 0) & (q < chips) & (d + 1 - side > 0) & held(q))
             def _():
+                for h in range(PARTS):
+                    arrived(q, 1 - core, h)
+
+                @pl.when(is_inner & (q == far))
+                def _():
+                    project_far()
+
                 project(q)
 
     @pl.loop(0, chips)
@@ -234,10 +322,14 @@
         for r in range(1, seq_count):
             gm_copy(q, peer(r), seq).wait_recv()
 
+        @pl.when(is_end & (q == far))
+        def _():
+            far_gm(seq, seq).wait_recv()
+
     def gi_copy(g, source, target):
         return pltpu.make_async_remote_copy(
             src_ref=gi_send.at[target, g],
-            dst_ref=gi_back.at[source, g],
+            dst_ref=gi_out.at[source, g],
             send_sem=gi_ssem.at[g, target],
             recv_sem=gi_rsem.at[g, source],
             device_id={"seq": target},
@@ -247,7 +339,7 @@
     def gf_copy(source, target):
         return pltpu.make_async_remote_copy(
             src_ref=gf_send.at[target],
-            dst_ref=gf_back.at[source],
+            dst_ref=gf_out.at[source],
             send_sem=gf_ssem.at[target],
             recv_sem=gf_rsem.at[source],
             device_id={"seq": target},
@@ -260,17 +352,17 @@
         fold = BLK // unit
         for a in range(count):
             for u in range(fold):
-                gm_rows[a * width : (a + 1) * width, u * unit : (u + 1) * unit] = gm_wide[
+                gm_rows[g, a * width : (a + 1) * width, u * unit : (u + 1) * unit] = gm_wide[
                     a * fold + u, pl.ds(first, width), :
                 ]
-        gm_rows[depth:, :] = jnp.zeros((gm_rows.shape[0] - depth, BLK), jnp.bfloat16)
+        gm_rows[g, depth:, :] = jnp.zeros((depth, BLK), jnp.bfloat16)
 
         step = min(4, count)
         total = None
         for j in range(0, count, step):
             m = (count - j) * width
             left = jnp.concatenate(
-                [gm_rows[(j + q) * width : (j + q) * width + m, :] for q in range(step)], axis=1
+                [gm_rows[g, (j + q) * width : (j + q) * width + m, :] for q in range(step)], axis=1
             )
             right = jnp.concatenate(
                 [
@@ -293,14 +385,17 @@
             ].astype(jnp.bfloat16)
         for r in range(1, seq_count):
             gi_copy(g, seq, peer(r)).start()
-        gi_back[seq, g] = gi_send[seq, g]
+        pltpu.make_async_copy(gi_send.at[seq, g], gi_out.at[seq, g], own_sem.at[g]).start()
+
+    @pl.loop(0, groups)
+    def _(g):
 
         prod[:, :HALF] = jnp.zeros((HALF, HALF), jnp.float32)
         for j in range(count):
             k = min(depth, -(-((count - j) * width) // BLK) * BLK)
             part = jnp.dot(
                 x_cols[g, :, :k],
-                gm_rows[j * width : j * width + k, :],
+                gm_rows[g, j * width : j * width + k, :],
                 preferred_element_type=jnp.float32,
             )
             lo = j * BLK
@@ -323,24 +418,17 @@
 
     for r in range(1, seq_count):
         gf_copy(seq, peer(r)).start()
-    gf_back[seq] = gf_send[seq]
+    own_gf = pltpu.make_async_copy(gf_send.at[seq], gf_out.at[seq], own_sem.at[groups])
+    own_gf.start()
 
     @pl.loop(0, groups)
     def _(g):
         for r in range(1, seq_count):
             gi_copy(g, peer(r), seq).wait_recv()
 
-    per_tile = max(1, HALF // own_ch)
-    for s in range(0, seq_count, per_tile):
-        tile = jnp.concatenate(
-            [gi_back[s + i, g] for i in range(per_tile) for g in range(groups)], axis=0
-        )
-        gi_out[:, s * own_ch : (s + per_tile) * own_ch] = tile.T
     for r in range(1, seq_count):
         gf_copy(peer(r), seq).wait_recv()
-    for s in range(seq_count):
-        for g in range(groups):
-            gf_out[s * groups + g : s * groups + g + 1, :] = gf_back[s, g]
+    own_gf.wait()
 
     for r in range(1, seq_count):
         x_copy(seq, peer(r)).wait_send()
@@ -350,21 +438,38 @@
     def _(g):
         for r in range(1, seq_count):
             gi_copy(g, seq, peer(r)).wait_send()
+        pltpu.make_async_copy(gi_send.at[seq, g], gi_out.at[seq, g], own_sem.at[g]).wait()
 
     @pl.loop(0, chips)
     def _(q):
-        for r in range(1, seq_count):
-            gm_copy(q, seq, peer(r)).wait_send()
+        @pl.when(held(q))
+        def _():
+            for r in range(1, seq_count):
+                gm_copy(q, seq, peer(r)).wait_send()
+            for h in range(PARTS):
+                hop(2, q, h, twin).wait_send()
+
         for h in range(PARTS):
-            hop(2, q, h, twin).wait_send()
-
-            @pl.when(has_up & (q <= spot))
+            @pl.when(has_up & (q <= spot) & held(q) & onward(q))
             def _():
                 hop(0, q, h, up).wait_send()
 
-            @pl.when(has_down & (q >= spot))
+            @pl.when(has_down & (q >= spot) & held(q) & onward(q))
             def _():
                 hop(1, q, h, down).wait_send()
+
+    @pl.when(is_end)
+    def _():
+        for h in range(far_parts):
+            far_hop(h).wait_send()
+
+    @pl.when(is_inner)
+    def _():
+        for r in range(1, seq_count):
+            for h in range(far_parts):
+                far_share(seq, peer(r), h).wait_send()
+        for r in range(seq_count):
+            far_gm(seq, peer(r)).wait_send()
 
 
 def on_device(chan_count, seq_count, conv_input, grad_out, out_weight, filters):
@@ -386,14 +491,14 @@
     hbm = pl.BlockSpec(memory_space=pl.ANY)
     vmem = pl.BlockSpec(memory_space=pltpu.VMEM)
     work = chans * rows * model // seq_count + 2 * own_ch * rows * rows
-    return pl.pallas_call(
+    through, lagged = pl.pallas_call(
         functools.partial(whole_kernel, chan_count, seq_count, width),
         out_shape=(
-            jax.ShapeDtypeStruct((span_t, chans), bf16),
-            jax.ShapeDtypeStruct((all_groups, cut), f32),
+            jax.ShapeDtypeStruct((seq_count, groups, width, span_t), bf16),
+            jax.ShapeDtypeStruct((seq_count, groups, 1, cut), f32),
         ),
         in_specs=[hbm, hbm, hbm, vmem],
-        out_specs=(vmem, vmem),
+        out_specs=(hbm, hbm),
         scratch_shapes=[
             pltpu.VMEM((chips, unit, model), bf16),
             pltpu.VMEM(out_weight.shape, bf16),
@@ -405,12 +510,17 @@
             pltpu.VMEM((groups, BLK, depth), bf16),
             pltpu.VMEM((chips, chans, unit), bf16),
             pltpu.VMEM((seq_count * chips, own_ch, unit), bf16),
-            pltpu.VMEM((2 * depth, BLK), bf16),
-            pltpu.VMEM((seq_count, groups, width, span_t), bf16),
+            pltpu.VMEM((groups, 2 * depth, BLK), bf16),
             pltpu.VMEM((seq_count, groups, width, span_t), bf16),
             pltpu.VMEM((HALF, rows + HALF), f32),
             pltpu.VMEM((seq_count, groups, 1, cut), f32),
-            pltpu.VMEM((seq_count, groups, 1, cut), f32),
+            pltpu.VMEM(out_weight.shape, bf16),
+            pltpu.VMEM((chans, unit), bf16),
+            dma((PARTS,)),
+            dma((seq_count, PARTS)),
+            dma((seq_count, PARTS)),
+            dma((seq_count,)),
+            dma((groups + 1,)),
             dma((3,)),
             dma((3, chips, PARTS)),
             dma((chips, 2, PARTS)),
@@ -430,6 +540,7 @@
             vmem_limit_bytes=56 * 1024 * 1024, collective_id=0, has_side_effects=True
         ),
     )(conv_input, grad_out, out_weight, filters)
+    return through.reshape(chans, span_t).T, lagged.reshape(all_groups, cut)
 
 
 def solution(mesh):

time: 107 us -> 100 us (0.935)
  Pallas kernels: 102 us -> 94.7 us
  other arithmetic: 0 us -> 1.25 us
    pallas_call x1, Pallas kernels: 102 us -> 94.7 us  [on_device(): pl.pallas_call(functools.partial(whole_kernel, chan_count, seq_count, wid...]
    unnamed x2 -> x0, local copies, waits for them, and re-layouts: 3.83 us -> none
    reshape x0 -> x2, local copies, waits for them, and re-layouts: none -> 2.98 us  [on_device(): return (through.reshape(chans, span_t).T, lagged.reshape(all_groups, cut))]
    pallas_call x0 -> x1, other arithmetic: none -> 1.25 us  [on_device(): pl.pallas_call(functools.partial(whole_kernel, chan_count, seq_count, wid...]
where the time goes in v3:
time: 100 us; the launch traced here: 99.5 us
  Pallas kernels  94.7 us (95%)
  local copies, waits for them, and re-layouts  2.98 us (3%)
  other arithmetic  1.25 us (1%)
    pallas_call x1, Pallas kernels, on_device(): pl.pallas_call(functools.partial(whole_kernel, chan_count, seq_count, wid...  94.7 us
    reshape x2, local copies, waits for them, and re-layouts, on_device(): return (through.reshape(chans, span_t).T, lagged.reshape(all_groups, cut))  2.98 us

profile of v3, /device:TPU:0, one launch (start us, length us, event | category | flops | bytes accessed | tf_op | source)
XLA Modules:
  0.0 99.5 jit_solution(285073179800461448)
XLA Ops:
  0.6 94.7 %shard_map.59 = (bf16[4,4,32,1024]{3,2,1,0:T(8,128)(2,1)}, f32[4,4,1,2048]{3,2,1,0:T(1,128)}) custom-call(bf16[1024,512]{1,0:T(8,128)(2,1)} %x_hbm.1, bf16[128,4096]{1,0:T(8,128)(2,1)} %go_hbm.1, bf16[512,4096]{1,0:T(8,128)(2,1)} %w_hbm.1, bf16[16,8192]{1,0:T(8,128)(2,1)} %f_ref.1), custom_call_target="tpu_custom_call" | custom-call | flops 12884901888 | bytes 16777216 | tf_op jit(solution)/shard_map/pallas_call | solution.py:494
  95.3 2.3 %copy.6 = bf16[512,1024]{0,1:T(8,128)(2,1)} copy(bf16[512,1024]{1,0:T(8,128)(2,1)} %bitcast.3) | data formatting | bytes 2097152 | tf_op jit(solution)/shard_map/reshape | solution.py:543
  97.6 1.2 %reduce = f32[4,4,2048]{2,1,0:T(4,128)S(1)} reduce(f32[4,4,1,2048]{3,2,1,0:T(1,128)} %get-tuple-element.5, f32[]{:T(128)} %constant), dimensions={2}, to_apply=%get-tuple-element.5.reduce_sub_computation | reduce | bytes 262148 | tf_op jit(solution)/shard_map/pallas_call | solution.py:494
  98.8 0.7 reshape.11

commit v4 on v3

--- a/solution.py
+++ b/solution.py
@@ -165,6 +165,11 @@
             device_id_type=MESH,
         )
 
+    @pl.when(is_end)
+    def _():
+        for h in range(far_parts):
+            far_hop(h).start()
+
     load_own.wait()
     for h in range(PARTS):
         @pl.when(has_up)
@@ -174,11 +179,6 @@
         @pl.when(has_down)
         def _():
             hop(1, spot, h, down).start()
-
-        if h < far_parts:
-            @pl.when(is_end)
-            def _():
-                far_hop(h).start()
 
     for h in range(PARTS):
         hop(2, spot, h, twin).start()
@@ -268,6 +268,13 @@
         x_cols[g] = x_rows.T
 
     def relay(d):
+        for h in range(far_parts):
+            @pl.when(is_inner & (d == 1))
+            def _():
+                far_hop(h).wait_recv()
+                for r in range(1, seq_count):
+                    far_share(seq, peer(r), h).start()
+
         for h in range(PARTS):
             @pl.when((spot >= d) & held(spot - d))
             def _():
@@ -288,13 +295,6 @@
                     hop(1, spot + d, h, down).start()
 
                 hop(2, spot + d, h, twin).start()
-
-            if h < far_parts:
-                @pl.when(is_inner & (d == 1))
-                def _():
-                    far_hop(h).wait_recv()
-                    for r in range(1, seq_count):
-                        far_share(seq, peer(r), h).start()
 
     @pl.loop(0, chips)
     def _(d):

time: 100 us -> 100 us (level)
  no operation moved by 1% of the time
where the time goes in v4:
time: 100 us; the launch traced here: 99.5 us
  Pallas kernels  94.6 us (95%)
  local copies, waits for them, and re-layouts  2.98 us (3%)
  other arithmetic  1.25 us (1%)
    pallas_call x1, Pallas kernels, on_device(): pl.pallas_call(functools.partial(whole_kernel, chan_count, seq_count, wid...  94.6 us
    reshape x2, local copies, waits for them, and re-layouts, on_device(): return (through.reshape(chans, span_t).T, lagged.reshape(all_groups, cut))  2.98 us

profile of v4, /device:TPU:0, one launch (start us, length us, event | category | flops | bytes accessed | tf_op | source)
XLA Modules:
  0.0 99.5 jit_solution(17236753574083932110)
XLA Ops:
  0.6 94.6 %shard_map.59 = (bf16[4,4,32,1024]{3,2,1,0:T(8,128)(2,1)}, f32[4,4,1,2048]{3,2,1,0:T(1,128)}) custom-call(bf16[1024,512]{1,0:T(8,128)(2,1)} %x_hbm.1, bf16[128,4096]{1,0:T(8,128)(2,1)} %go_hbm.1, bf16[512,4096]{1,0:T(8,128)(2,1)} %w_hbm.1, bf16[16,8192]{1,0:T(8,128)(2,1)} %f_ref.1), custom_call_target="tpu_custom_call" | custom-call | flops 12884901888 | bytes 16777216 | tf_op jit(solution)/shard_map/pallas_call | solution.py:494
  95.3 2.3 %copy.6 = bf16[512,1024]{0,1:T(8,128)(2,1)} copy(bf16[512,1024]{1,0:T(8,128)(2,1)} %bitcast.3) | data formatting | bytes 2097152 | tf_op jit(solution)/shard_map/reshape | solution.py:543
  97.6 1.2 %reduce = f32[4,4,2048]{2,1,0:T(4,128)S(1)} reduce(f32[4,4,1,2048]{3,2,1,0:T(1,128)} %get-tuple-element.5, f32[]{:T(128)} %constant), dimensions={2}, to_apply=%get-tuple-element.5.reduce_sub_computation | reduce | bytes 262148 | tf_op jit(solution)/shard_map/pallas_call | solution.py:494
  98.8 0.7 reshape.11
